TPU v7x, 32 devices: a whole 2x2x4 slice. The times are simulated.
32 devices in a mesh: groups: 2 (over y), col: 4 (over z), row: 4 (over x, core).
Axes of the slice: x: 2, y: 2, z: 4, core: 2. Of those that a mesh axis runs over, the one named last changes fastest.
Arguments:
- pair_slab: bfloat16 [128, 512, 128], P(('groups', 'row'), 'col'), parts along dimension 0, may hold values from -6 to 6
- tile_pair: bfloat16 [8, 2, 128, 128, 128], P(('groups', 'col'), None, 'row'), parts along dimension 0, may hold values from -6 to 6
- tile_cotan: bfloat16 [8, 2, 128, 128, 128], P(('groups', 'col'), None, 'row'), parts along dimension 0, may hold values from -6 to 6
- tile_rows: int32 [8, 2], P(('groups', 'col')), parts along dimension 0, may hold values from 0 to 3, as said below
- tile_count: int32 [8], P(('groups', 'col')), parts along dimension 0, may hold values from 1 to 2, as said below
- norm_gain: float32 [128], replicated, may hold values from 0.5 to 1.5
- norm_bias: float32 [128], replicated, may hold values from -2.5 to 2.5
- w_in: bfloat16 [128, 512], replicated, may hold values from -0.5 to 0.5
- out_gain: float32 [128], replicated, may hold values from 0.5 to 1.5
- out_bias: float32 [128], replicated, may hold values from -2.5 to 2.5
- w_out: bfloat16 [128, 128], replicated, may hold values from -0.5 to 0.5
- w_gate: bfloat16 [128, 128], replicated, may hold values from -0.5 to 0.5
Outputs:
- update: bfloat16 [8, 2, 128, 128, 128], P(('groups', 'col'), None, 'row'), parts along dimension 0
- grad_slab: bfloat16 [128, 512, 128], P(('groups', 'row'), 'col'), parts along dimension 0
- grad_tiles: bfloat16 [8, 2, 128, 128, 128], P(('groups', 'col'), None, 'row'), parts along dimension 0
- grad_in_w: float32 [256, 512], P('groups'), parts along dimension 0
- grad_out_w: float32 [256, 128], P('groups'), parts along dimension 0
- grad_gate_w: float32 [256, 128], P('groups'), parts along dimension 0
There are 2 independent parts, one for each index of `groups`. A program takes and returns all parts, laid end to end along the dimension named above; an argument that names none is the same for every part. Nothing has to cross between parts.
Inputs may be any that keep to these rules, and one draw needn't show every extreme that they name: `tile_count`: every column block has at least one active slot and some column block has all 2 active. `tile_rows`: the row blocks named by the slots of one column block are distinct; slots at or past the count are inactive.
All inputs are finite; a program needn't handle non-finite values.
Results may differ from a plain program's by a relative error of at most 0.015.
Values may be sent and summed in bfloat16 or wider, within the bound.
A program may use at most 128 MiB of HBM per device.

v0:
```python
import jax
import jax.numpy as jnp
from jax import lax
from jax.sharding import PartitionSpec as P

epsilon = 1e-05


def normalize(values):
    center = values - jnp.mean(values, axis=-1, keepdims=True)
    variance = jnp.mean(center * center, axis=-1, keepdims=True)
    inverse = lax.rsqrt(variance + epsilon)
    return (center * inverse, inverse)


def norm_back(grad_in, centred, inverse, gain):
    scaled = grad_in * gain
    first = jnp.mean(scaled, axis=-1, keepdims=True)
    second = jnp.mean(scaled * centred, axis=-1, keepdims=True)
    return inverse * (scaled - first - centred * second)


def rounded(values):
    return lax.optimization_barrier(values.astype(jnp.bfloat16)).astype(jnp.float32)


def body(
    pair_slab,
    tile_pair,
    tile_cotan,
    tile_rows,
    tile_count,
    norm_gain,
    norm_bias,
    w_in,
    out_gain,
    out_bias,
    w_out,
    w_gate,
):
    k_local, tile_len, channels = pair_slab.shape
    hidden_w = w_out.shape[0]
    slots = tile_rows.shape[1]
    row_count = lax.axis_size("row")
    col_count = lax.axis_size("col")
    row_part = tile_len // row_count
    slab_hat, slab_inv = normalize(pair_slab.astype(jnp.float32))
    slab_norm = (slab_hat * norm_gain + norm_bias).astype(jnp.bfloat16)
    flat_norm = slab_norm.reshape(-1, channels)
    project = jnp.dot(flat_norm, w_in, preferred_element_type=jnp.float32).reshape(
        k_local, tile_len, 4 * hidden_w
    )
    left_proj = project[..., :hidden_w]
    left_sig = jax.nn.sigmoid(project[..., hidden_w : 2 * hidden_w])
    right_proj = project[..., 2 * hidden_w : 3 * hidden_w]
    right_sig = jax.nn.sigmoid(project[..., 3 * hidden_w :])
    left_edges = (left_sig * left_proj).astype(jnp.bfloat16)
    right_edges = (right_sig * right_proj).astype(jnp.bfloat16)
    row_blocks = tile_rows[0]
    active = (jnp.arange(slots) < tile_count[0]).astype(jnp.float32)
    selector = (row_blocks[:, None] == jnp.arange(col_count)[None, :]).astype(jnp.float32) * active[
        :, None
    ]
    spread = lax.all_to_all(
        left_edges.reshape(k_local, row_count, row_part, hidden_w),
        "row",
        split_axis=1,
        concat_axis=0,
        tiled=True,
    )
    panels = lax.all_gather(spread, "col", axis=1, tiled=True)
    chosen = jnp.take(panels, row_blocks, axis=1)
    right_full = lax.all_gather(right_edges, "row", axis=0, tiled=True)
    grouped = jnp.einsum(
        "gksih,gkjh->gsijh",
        chosen.reshape(row_count, k_local, slots, row_part, hidden_w),
        right_full.reshape(row_count, k_local, tile_len, hidden_w),
        preferred_element_type=jnp.float32,
    )
    combined = jnp.sum(rounded(grouped), axis=0)
    comb_hat, comb_inv = normalize(combined)
    comb_norm = (comb_hat * out_gain + out_bias).astype(jnp.bfloat16)
    pair_hat, pair_inv = normalize(tile_pair[0].astype(jnp.float32))
    pair_norm = (pair_hat * norm_gain + norm_bias).astype(jnp.bfloat16)
    flat_comb = comb_norm.reshape(-1, hidden_w)
    flat_pair = pair_norm.reshape(-1, channels)
    mixed = jnp.dot(flat_comb, w_out, preferred_element_type=jnp.float32)
    gate = jax.nn.sigmoid(jnp.dot(flat_pair, w_gate, preferred_element_type=jnp.float32))
    row_mask = jnp.repeat(active, row_part * tile_len)[:, None]
    update = (row_mask * gate * mixed).astype(jnp.bfloat16)
    cotan = tile_cotan[0].astype(jnp.float32).reshape(-1, channels) * row_mask
    grad_mixed = (cotan * gate).astype(jnp.bfloat16)
    grad_logit = (cotan * mixed * gate * (1.0 - gate)).astype(jnp.bfloat16)
    grad_out_w = jnp.dot(flat_comb.T, grad_mixed, preferred_element_type=jnp.float32)
    grad_gate_w = jnp.dot(flat_pair.T, grad_logit, preferred_element_type=jnp.float32)
    out_total, gate_total = (grad_out_w, grad_gate_w)
    grad_comb = jnp.dot(grad_mixed, w_out.T, preferred_element_type=jnp.float32).reshape(
        slots, row_part, tile_len, hidden_w
    )
    grad_pair = jnp.dot(grad_logit, w_gate.T, preferred_element_type=jnp.float32).reshape(
        slots, row_part, tile_len, channels
    )
    pair_back = norm_back(grad_pair, pair_hat, pair_inv, norm_gain).astype(jnp.bfloat16)
    comb_back = norm_back(grad_comb, comb_hat, comb_inv, out_gain).astype(jnp.bfloat16)
    left_term = rounded(
        jnp.einsum("sijh,kjh->ksih", comb_back, right_full, preferred_element_type=jnp.float32)
    )
    routed = jnp.einsum("ksih,sb->kbih", left_term, selector)
    column_sum = lax.psum_scatter(
        routed.astype(jnp.bfloat16), "col", scatter_dimension=1, tiled=True
    ).astype(jnp.float32)
    returned = lax.all_to_all(
        column_sum.reshape(row_count, k_local, row_part, hidden_w).astype(jnp.bfloat16),
        "row",
        split_axis=0,
        concat_axis=2,
        tiled=True,
    ).astype(jnp.float32)
    left_grad = returned.reshape(k_local, tile_len, hidden_w)
    right_part = jnp.einsum(
        "sijh,ksih->skjh", comb_back, chosen, preferred_element_type=jnp.float32
    )
    right_grad = jnp.sum(
        lax.psum_scatter(
            right_part.astype(jnp.bfloat16), "row", scatter_dimension=1, tiled=True
        ).astype(jnp.float32),
        axis=0,
    )
    grad_project = jnp.concatenate(
        [
            left_grad * left_sig,
            left_grad * left_proj * left_sig * (1.0 - left_sig),
            right_grad * right_sig,
            right_grad * right_proj * right_sig * (1.0 - right_sig),
        ],
        axis=-1,
    ).astype(jnp.bfloat16)
    flat_grad = grad_project.reshape(-1, 4 * hidden_w)
    grad_in_w = jnp.dot(flat_norm.T, flat_grad, preferred_element_type=jnp.float32)
    grad_norm = jnp.dot(flat_grad, w_in.T, preferred_element_type=jnp.float32).reshape(
        k_local, tile_len, channels
    )
    grad_slab = norm_back(grad_norm, slab_hat, slab_inv, norm_gain).astype(jnp.bfloat16)
    in_total, out_total, gate_total = lax.psum((grad_in_w, out_total, gate_total), ("col", "row"))
    update_out = update.reshape(1, slots, row_part, tile_len, channels)
    tiles_out = pair_back.reshape(1, slots, row_part, tile_len, channels)
    return (update_out, grad_slab, tiles_out, in_total, out_total, gate_total)


def solution(mesh):
    return jax.shard_map(
        body,
        mesh=mesh,
        in_specs=(
            P(("groups", "row"), "col", None),
            P(("groups", "col"), None, "row", None, None),
            P(("groups", "col"), None, "row", None, None),
            P(("groups", "col"), None),
            P(("groups", "col")),
            P(),
            P(),
            P(),
            P(),
            P(),
            P(),
            P(),
        ),
        out_specs=(
            P(("groups", "col"), None, "row", None, None),
            P(("groups", "row"), "col", None),
            P(("groups", "col"), None, "row", None, None),
            P("groups", None),
            P("groups", None),
            P("groups", None),
        ),
        check_vma=False,
    )
```

profile of v0, /device:TPU:0, one launch (start us, length us, event | category | flops | bytes accessed | tf_op | source)
XLA Modules:
  0.0 365.0 jit_solution(873537648331085904)
XLA Ops:
  14.5 4.2 %all-to-all-start = ((bf16[16,4,32,128]{3,2,0,1:T(8,128)(2,1)}), bf16[16,4,32,128]{3,2,0,1:T(8,128)(2,1)S(1)}, u32[]{:S(2)}, u32[]{:S(2)}) async-start(bf16[16,4,32,128]{3,2,0,1:T(8,128)(2,1)} %copy.57), calls=%async_computation | async-start | bytes 1048576 | tf_op jit(solution)/shard_map/all_to_all | solution.py:64
  19.5 9.8 %all-to-all-done = bf16[16,4,32,128]{3,2,0,1:T(8,128)(2,1)S(1)} async-done(((bf16[16,4,32,128]{3,2,0,1:T(8,128)(2,1)}), bf16[16,4,32,128]{3,2,0,1:T(8,128)(2,1)S(1)}, u32[]{:S(2)}, u32[]{:S(2)}) %all-to-all-start) | async-done | bytes 524320 | tf_op jit(solution)/shard_map/all_to_all | solution.py:64
  33.4 3.5 add_convert_fusion.1
  36.9 3.4 all-gather.3.cloned.1.call-done
  40.3 4.5 %copy.74 = bf16[4,16,128,128,1]{2,1,4,3,0:T(8,128)(2,1)} copy(bf16[4,16,128,128,1]{3,2,1,0,4:T(8,128)(2,1)} %bitcast.112) | data formatting | bytes 4194304 | tf_op jit(solution)/shard_map/reshape | solution.py:77
  44.8 4.2 %copy.75 = bf16[64,128,128,1]{1,0,3,2:T(8,128)(2,1)} copy(bf16[64,128,128,1]{2,1,0,3:T(8,128)(2,1)} %bitcast.113) | data formatting | bytes 4194304 | tf_op jit(solution)/shard_map/all_gather | solution.py:73
  49.0 40.4 %all-gather.5.cloned.1.call-done = bf16[64,4,32,128]{3,2,1,0:T(8,128)(2,1)} async-done(((bf16[64,1,32,128]{3,2,1,0:T(8,128)(2,1)}), bf16[64,4,32,128]{3,2,1,0:T(8,128)(2,1)}) %all-gather.5.cloned.1.call-update) | async-done | bytes 2097168 | tf_op jit(solution)/shard_map/all_gather | solution.py:71
  89.5 3.3 gather_fusion
  95.2 7.2 %copy.61 = bf16[4,16,2,32,128]{3,1,2,4,0:T(8,128)(2,1)} copy(bf16[4,16,2,32,128]{4,3,2,1,0:T(8,128)(2,1)} %broadcast_select_fusion.1) | data formatting | bytes 2097152 | tf_op jit(solution)/shard_map/jit(_take)/select_n | solution.py:72
  102.4 5.2 %convert_bitcast_fusion = bf16[4,2,32,128,128]{3,2,1,4,0:T(8,128)(2,1)S(1)} fusion(bf16[4,16,128,128,1]{2,1,4,3,0:T(8,128)(2,1)} %copy.74, bf16[4,16,2,32,128]{3,1,2,4,0:T(8,128)(2,1)} %copy.61), kind=kOutput, calls=%fused_computation.7 | convolution fusion | flops 138412032 | bytes 11534336 | tf_op jit(solution)/shard_map/gksih,gkjh->gsijh/dot_general | solution.py:74
  107.7 5.1 %convert_reduce_fusion = (f32[2,32,128]{2,1,0:T(8,128)S(1)}, f32[2,32,128,128]{2,1,0,3:T(8,128)}) fusion(bf16[4,2,32,128,128]{3,2,1,4,0:T(8,128)(2,1)S(1)} %convert_bitcast_fusion), kind=kLoop, calls=%fused_computation.1 | loop fusion | flops 11526144 | bytes 12615680 | tf_op jit(solution)/shard_map/reduce_sum | solution.py:10
  112.7 5.3 %copy.62 = f32[2,32,128,128]{3,2,1,0:T(8,128)} copy(f32[2,32,128,128]{2,1,0,3:T(8,128)} %get-tuple-element.31) | data formatting | bytes 8388608 | tf_op jit(solution)/shard_map/reduce_sum | solution.py:80
  118.1 2.8 multiply_reduce_fusion.2
  121.5 4.5 %add_convert_fusion = bf16[8192,128]{1,0:T(8,128)(2,1)S(1)} fusion(f32[2,32,128,128]{3,2,1,0:T(8,128)S(1)} %copy-done.2, f32[128]{0:T(128)S(1)} %copy-done.18, f32[128]{0:T(128)S(1)} %copy-done.15, f32[8192]{0:T(1024)S(1)} %bitcast.123, f32[8192]{0:T(1024)S(1)} %bitcast.119), kind=kLoop, calls=%fused_computation.28 | loop fusion | flops 5242880 | bytes 6358016 | tf_op jit(solution)/shard_map/convert_element_type | solution.py:82
  129.1 4.3 %fusion.8 = (bf16[8192,128]{1,0:T(8,128)(2,1)}, bf16[8192,128]{1,0:T(8,128)(2,1)}, bf16[8192,128]{1,0:T(8,128)(2,1)S(1)}) fusion(f32[8192,128]{1,0:T(8,128)S(1)} %fusion.48, bf16[1,2,32,128,128]{4,3,2,1,0:T(8,128)(2,1)S(1)} %copy-done.19, f32[8192]{0:T(1024)S(1)} %bitcast.132, bf16[8192,128]{1,0:T(8,128)(2,1)S(1)} %copy-done.7, ...), kind=kOutput, calls=%fused_computation.14 | convolution fusion | flops 284164096 | bytes 14745600 | tf_op jit(solution)/shard_map/dot_general | solution.py:88
  133.4 6.2 %multiply_reduce_fusion.4 = (f32[8192]{0:T(1024)S(1)}, f32[8192]{0:T(1024)S(1)}, f32[8192,128]{1,0:T(8,128)}) fusion(f32[128]{0:T(128)S(1)} %copy-done.15, f32[8192]{0:T(1024)S(1)} %bitcast.124, f32[8192]{0:T(1024)S(1)} %bitcast.120, f32[2,32,128,128]{3,2,1,0:T(8,128)S(1)} %copy-done.2, bf16[8192,128]{1,0:T(8,128)(2,1)S(1)} %get-tuple-element.43, ...), kind=kOutput, calls=%fused_computation.32 | convolution fusion | flops 274710528 | bytes 10650112 | tf_op jit(solution)/shard_map/dot_general | solution.py:97
  139.6 5.5 %copy.63 = f32[2,32,128,128]{2,1,0,3:T(8,128)} copy(f32[2,32,128,128]{3,2,1,0:T(8,128)} %bitcast.110) | data formatting | bytes 8388608 | tf_op jit(solution)/shard_map/reshape | solution.py:97
  145.1 4.8 %multiply_convert_fusion.1 = bf16[2,32,128,128]{2,1,0,3:T(8,128)(2,1)S(1)} fusion(f32[2,32,128,128]{2,1,0,3:T(8,128)} %copy.63, f32[2,32,128,128]{2,1,0,3:T(8,128)} %get-tuple-element.31, f32[2,32,128]{2,1,0:T(8,128)S(1)} %bitcast.128, f32[2,32,128]{2,1,0:T(8,128)S(1)} %bitcast.129, f32[128]{0:T(128)S(1)} %copy-done.15, f32[2,32,128]{2,1,0:T(8,128)S(1)} %add_rsqrt_fusion, ...), kind=kLoop, calls=%fused_computation.25 | loop fusion | flops 8388608 | bytes 10617344 | tf_op jit(solution)/shard_map/convert_element_type | solution.py:104
  151.3 2.5 convert_bitcast_fusion.3
  153.8 4.7 %copy.65 = bf16[64,2,32,128]{3,1,2,0:T(2,128)(2,1)} copy(bf16[64,2,32,128]{0,2,1,3:T(8,128)(2,1)} %convert_bitcast_fusion.3) | data formatting | bytes 2097152 | tf_op jit(solution)/shard_map/optimization_barrier | solution.py:24
  158.5 2.8 convert_bitcast_fusion.2
  165.4 5.4 %copy.68 = bf16[64,2,32,128]{0,2,3,1:T(8,128)(2,1)} copy(bf16[64,2,32,128]{3,2,0,1:T(8,128)(2,1)} %broadcast_select_fusion) | data formatting | bytes 2097152 | tf_op jit(solution)/shard_map/jit(_take)/select_n | solution.py:72
  170.8 5.5 %convert_bitcast_fusion.1 = bf16[2,64,128,128]{2,1,3,0:T(8,128)(2,1)} fusion(bf16[64,2,32,128]{0,2,3,1:T(8,128)(2,1)} %copy.68, bf16[2,32,128,128]{2,1,0,3:T(8,128)(2,1)} %copy-done.5), kind=kOutput, calls=%fused_computation.24 | convolution fusion | flops 136314880 | bytes 7340032 | tf_op jit(solution)/shard_map/sijh,ksih->skjh/dot_general | solution.py:120
  176.3 7.2 %multiply_reduce_fusion.3 = (f32[8192]{0:T(1024)S(1)}, f32[8192]{0:T(1024)S(1)}, f32[8192,128]{1,0:T(8,128)S(1)}) fusion(f32[128]{0:T(128)S(1)} %copy-done.16, f32[8192]{0:T(1024)S(1)} %bitcast.127, f32[8192]{0:T(1024)S(1)} %bitcast.122, bf16[1,2,32,128,128]{4,3,2,1,0:T(8,128)(2,1)S(1)} %copy-done.3, bf16[8192,128]{1,0:T(8,128)(2,1)} %get-tuple-element.41, ...), kind=kOutput, calls=%fused_computation.31 | convolution fusion | flops 275759104 | bytes 8552960 | tf_op jit(solution)/shard_map/dot_general | solution.py:100
  183.5 5.9 %multiply_convert_fusion = bf16[1,2,32,128,128]{4,3,2,1,0:T(8,128)(2,1)} fusion(f32[1,2,32,128,128]{4,3,2,1,0:T(8,128)S(1)} %bitcast.115, bf16[1,2,32,128,128]{4,3,2,1,0:T(8,128)(2,1)S(1)} %copy-done.3, f32[2,32,128]{2,1,0:T(8,128)S(1)} %bitcast.130, f32[2,32,128]{2,1,0:T(8,128)S(1)} %broadcast_multiply_fusion.5, f32[2,32,128]{2,1,0:T(8,128)S(1)} %bitcast.131, ...), kind=kLoop, calls=%fused_computation.22 | loop fusion | flops 9437184 | bytes 8520192 | tf_op jit(solution)/shard_map/convert_element_type | solution.py:103
  189.5 16.3 %reduce-scatter.3.cloned.1.call-done = bf16[64,1,32,128]{3,2,0,1:T(8,128)(2,1)} async-done(((bf16[64,4,32,128]{3,2,0,1:T(8,128)(2,1)}), bf16[64,1,32,128]{3,2,0,1:T(8,128)(2,1)}) %reduce-scatter.3.cloned.1.call-update) | async-done | bytes 524304 | tf_op jit(solution)/shard_map/reduce_scatter | solution.py:109
  205.8 3.5 all-to-all-start.1
  209.6 3.8 %fusion.49 = f32[128,128]{1,0:T(8,128)} fusion(bf16[8192,128]{1,0:T(8,128)(2,1)} %copy-done.4, bf16[8192,128]{1,0:T(8,128)(2,1)} %copy-done.9), kind=kOutput, calls=%fused_computation.105 | convolution fusion | flops 268435456 | bytes 4259840 | tf_op jit(solution)/shard_map/dot_general | solution.py:94
  214.7 3.4 all-to-all-done.1
  218.3 33.9 %reduce-scatter.5.cloned.1.call-done = bf16[2,16,128,128]{2,1,3,0:T(8,128)(2,1)} async-done(((bf16[2,64,128,128]{2,1,3,0:T(8,128)(2,1)}), bf16[2,16,128,128]{2,1,3,0:T(8,128)(2,1)}) %reduce-scatter.5.cloned.1.call-update) | async-done | bytes 1048592 | tf_op jit(solution)/shard_map/reduce_scatter | solution.py:124
  255.0 3.6 multiply_convert_fusion.6
  264.0 89.8 %all-reduce.3.cloned.1.call-done = (f32[128,512]{1,0:T(8,128)}, f32[128,128]{1,0:T(8,128)}, f32[128,128]{1,0:T(8,128)}) async-done(((f32[128,512]{1,0:T(8,128)}, f32[128,128]{1,0:T(8,128)}, f32[128,128]{1,0:T(8,128)}), (f32[128,512]{1,0:T(8,128)}, f32[128,128]{1,0:T(8,128)}, f32[128,128]{1,0:T(8,128)})) %all-reduce.3.cloned.1.call-update) | async-done | bytes 393232 | tf_op jit(solution)/shard_map/psum | solution.py:144
  (95 shorter events, 37.7 us)
Async XLA Ops:
  7.2 1.7 copy-start
  7.2 33.2 %all-gather.3.cloned.1.call-start = ((), (), s32[]{:S(2)}) async-start(), calls=%async_computation.4 | async-start | bytes 2621440 | tf_op jit(solution)/shard_map/all_gather | solution.py:73
  10.4 1.9 copy-start.1
  12.3 7.2 %copy-start.21 = (s32[1,2]{1,0:T(1,128)S(1)}, s32[1,2]{1,0:T(1,128)}, u32[]{:S(2)}) copy-start(s32[1,2]{1,0:T(1,128)} %param.15) | copy-start | bytes 28
  12.3 17.9 %copy-start.3 = (bf16[1,2,32,128,128]{4,3,2,1,0:T(8,128)(2,1)S(1)}, bf16[1,2,32,128,128]{4,3,2,1,0:T(8,128)(2,1)}, u32[]{:S(2)}) copy-start(bf16[1,2,32,128,128]{4,3,2,1,0:T(8,128)(2,1)} %param.13) | copy-start | bytes 6291460
  13.7 19.8 %copy-start.16 = (f32[128]{0:T(128)S(1)}, f32[128]{0:T(128)}, u32[]{:S(2)}) copy-start(f32[128]{0:T(128)} %param.17) | copy-start | bytes 1540
  13.7 19.8 %copy-start.17 = (f32[128]{0:T(128)S(1)}, f32[128]{0:T(128)}, u32[]{:S(2)}) copy-start(f32[128]{0:T(128)} %param.18) | copy-start | bytes 1540
  14.5 14.8 %all-to-all-start = ((bf16[16,4,32,128]{3,2,0,1:T(8,128)(2,1)}), bf16[16,4,32,128]{3,2,0,1:T(8,128)(2,1)S(1)}, u32[]{:S(2)}, u32[]{:S(2)}) async-start(bf16[16,4,32,128]{3,2,0,1:T(8,128)(2,1)} %copy.57), calls=%async_computation | async-start | bytes 1048576 | tf_op jit(solution)/shard_map/all_to_all | solution.py:64
  18.7 70.7 %all-gather.5.cloned.1.call-start = ((), (), s32[]{:S(2)}) async-start(), calls=%async_computation.5 | async-start | bytes 2621440 | tf_op jit(solution)/shard_map/all_gather | solution.py:71
  29.3 0.8 copy-start.11
  30.1 175.6 %reduce-scatter.3.cloned.1.call-start = ((), (), s32[]{:S(2)}) async-start(), calls=%async_computation.6 | async-start | bytes 2621440 | tf_op jit(solution)/shard_map/reduce_scatter | solution.py:109
  118.1 3.4 copy-start.2
  118.1 3.4 copy-start.15
  118.1 3.5 copy-start.18
  120.9 5.2 %copy-start.14 = (bf16[128,128]{1,0:T(8,128)(2,1)S(1)}, bf16[128,128]{1,0:T(8,128)(2,1)}, u32[]{:S(2)}) copy-start(bf16[128,128]{1,0:T(8,128)(2,1)} %param.22) | copy-start | bytes 98308
  126.1 1.3 copy-start.4
  126.1 2.3 copy-start.7
  126.1 3.0 copy-start.19
  126.1 3.0 copy-start.20
  133.4 6.2 %copy-start.9 = (bf16[8192,128]{1,0:T(8,128)(2,1)}, bf16[8192,128]{1,0:T(8,128)(2,1)S(1)}, u32[]{:S(2)}) copy-start(bf16[8192,128]{1,0:T(8,128)(2,1)S(1)} %get-tuple-element.43) | copy-start | bytes 6291460
  145.1 6.2 %copy-start.6 = (bf16[64,128,128,1]{1,0,3,2:T(8,128)(2,1)S(1)}, bf16[64,128,128,1]{1,0,3,2:T(8,128)(2,1)}, u32[]{:S(2)}) copy-start(bf16[64,128,128,1]{1,0,3,2:T(8,128)(2,1)} %copy.75) | copy-start | bytes 6291460
  149.9 1.4 copy-start.5
  163.0 89.1 %reduce-scatter.5.cloned.1.call-start = ((), (), s32[]{:S(2)}) async-start(), calls=%async_computation.7 | async-start | bytes 5242880 | tf_op jit(solution)/shard_map/reduce_scatter | solution.py:124
  189.5 23.9 %copy-start.8 = (bf16[8192,128]{1,0:T(8,128)(2,1)S(1)}, bf16[8192,128]{1,0:T(8,128)(2,1)}, u32[]{:S(2)}) copy-start(bf16[8192,128]{1,0:T(8,128)(2,1)} %add_convert_fusion.1) | copy-start | bytes 6291460
  205.8 12.3 %all-to-all-start.1 = ((bf16[4,16,32,128]{3,2,1,0:T(8,128)(2,1)}), bf16[4,16,32,128]{3,2,1,0:T(8,128)(2,1)S(1)}, u32[]{:S(2)}, u32[]{:S(2)}) async-start(bf16[4,16,32,128]{3,2,1,0:T(8,128)(2,1)} %bitcast.125), calls=%async_computation.2 | async-start | bytes 1048576 | tf_op jit(solution)/shard_map/all_to_all | solution.py:112
  209.2 144.6 %all-reduce.3.cloned.1.call-start = ((), (), s32[]{:S(2)}) async-start(), calls=%async_computation.8 | async-start | bytes 786432 | tf_op jit(solution)/shard_map/psum | solution.py:144
  209.5 3.8 %copy-start.10 = (bf16[8192,128]{1,0:T(8,128)(2,1)S(1)}, bf16[8192,128]{1,0:T(8,128)(2,1)}, u32[]{:S(2)}) copy-start(bf16[8192,128]{1,0:T(8,128)(2,1)} %get-tuple-element.41) | copy-start | bytes 6291460
  258.6 0.8 copy-start.13
  258.7 2.0 copy-start.12
Sparse Core Ops, SparseCore 0:
  13.8 26.4 all-gather.2
  42.5 46.9 all-gather.4
  163.1 42.5 reduce-scatter.2
  208.3 43.8 reduce-scatter.4
  262.8 90.9 all-reduce.2
where the time goes:
time: 366 us; the launch traced here: 365 us
  waiting for transfers between devices  197 us (54%)
  local copies, waits for them, and re-layouts  60.2 us (16%)
  matrix products  44.3 us (12%)
  other arithmetic  40.4 us (11%)
  between operations  14.8 us (4%)
  starting transfers between devices  8.1 us (2%)
    psum x1, waiting for transfers between devices, body(): lax.psum((grad_in_w, out_total, gate_total), ('col', 'row'))  89.8 us
    all_gather x1, waiting for transfers between devices, body(): panels = lax.all_gather(spread, 'col', axis=1, tiled=True)  40.4 us
    reduce_scatter x1, waiting for transfers between devices, body(): lax.psum_scatter(right_part.astype(jnp.bfloat16), 'row', scatter_dimensio...  33.9 us
    reduce_scatter x1, waiting for transfers between devices, body(): lax.psum_scatter(routed.astype(jnp.bfloat16), 'col', scatter_dimension=1,...  16.3 us
    unnamed x51, local copies, waits for them, and re-layouts  14.8 us
    select_n x2, local copies, waits for them, and re-layouts, body(): chosen = jnp.take(panels, row_blocks, axis=1)  12.6 us
    all_to_all x1, waiting for transfers between devices, body(): lax.all_to_all(left_edges.reshape(k_local, row_count, row_part, hidden_w)...  9.82 us
  transfers between devices with their start and end apart: 7, of which 7 were waited for; matrix products, arithmetic and copies ran while one was open for 14% of the time, Pallas kernels for 0%

commit v1 on v0

--- a/solution.py
+++ b/solution.py
@@ -61,13 +61,20 @@
     selector = (row_blocks[:, None] == jnp.arange(col_count)[None, :]).astype(jnp.float32) * active[
         :, None
     ]
-    spread = lax.all_to_all(
-        left_edges.reshape(k_local, row_count, row_part, hidden_w),
-        "row",
-        split_axis=1,
-        concat_axis=0,
-        tiled=True,
-    )
+    x = left_edges.reshape(k_local, row_count, row_part, hidden_w)
+    ways, here = (lax.axis_size("row"), lax.axis_index("row"))
+    width = x.shape[1] // ways
+    dims = list(x.shape)
+    dims[1] = width
+    height = dims[0]
+    dims[0] = height * ways
+    full = jnp.zeros(dims, x.dtype)
+    for mask in range(ways):
+        part = lax.dynamic_slice_in_dim(x, (here ^ mask) * width, width, axis=1)
+        if mask:
+            part = lax.ppermute(part, "row", [(d, d ^ mask) for d in range(ways)])
+        full = lax.dynamic_update_slice_in_dim(full, part, (here ^ mask) * height, axis=0)
+    spread = full
     panels = lax.all_gather(spread, "col", axis=1, tiled=True)
     chosen = jnp.take(panels, row_blocks, axis=1)
     right_full = lax.all_gather(right_edges, "row", axis=0, tiled=True)

time: 366 us -> 364 us (level)
  waiting for transfers between devices: 197 us -> 192 us
    all_to_all x1 -> x0, waiting for transfers between devices: 9.82 us -> none  [body(): lax.all_to_all(left_edges.reshape(k_local, row_count, row_part, hidden_w)...]
    all_to_all x1 -> x0, starting transfers between devices: 4.21 us -> none  [body(): lax.all_to_all(left_edges.reshape(k_local, row_count, row_part, hidden_w)...]
    ppermute x0 -> x3, waiting for transfers between devices: none -> 3.9 us  [body(): part = lax.ppermute(part, 'row', [(d, d ^ mask) for d in range(ways)])]
  transfers between devices with their start and end apart: 7 -> 9, of which waited for: 7 -> 8; matrix products, arithmetic and copies ran while one was open for 14% -> 15% of each run, Pallas kernels for 0% -> 0%
where the time goes in v1:
time: 364 us; the launch traced here: 363 us
  waiting for transfers between devices  192 us (53%)
  local copies, waits for them, and re-layouts  62.8 us (17%)
  matrix products  44.3 us (12%)
  other arithmetic  42.4 us (12%)
  between operations  14.8 us (4%)
  starting transfers between devices  7.02 us (2%)
    psum x1, waiting for transfers between devices, body(): lax.psum((grad_in_w, out_total, gate_total), ('col', 'row'))  89.8 us
    all_gather x1, waiting for transfers between devices, body(): panels = lax.all_gather(spread, 'col', axis=1, tiled=True)  39.8 us
    reduce_scatter x1, waiting for transfers between devices, body(): lax.psum_scatter(right_part.astype(jnp.bfloat16), 'row', scatter_dimensio...  33.9 us
    reduce_scatter x1, waiting for transfers between devices, body(): lax.psum_scatter(routed.astype(jnp.bfloat16), 'col', scatter_dimension=1,...  15.6 us
    unnamed x51, local copies, waits for them, and re-layouts  15.4 us
    select_n x2, local copies, waits for them, and re-layouts, body(): chosen = jnp.take(panels, row_blocks, axis=1)  12.6 us
  transfers between devices with their start and end apart: 9, of which 8 were waited for; matrix products, arithmetic and copies ran while one was open for 15% of the time, Pallas kernels for 0%

profile of v1, /device:TPU:0, one launch (start us, length us, event | category | flops | bytes accessed | tf_op | source)
XLA Modules:
  0.0 363.2 jit_solution(826310761054450333)
XLA Ops:
  15.8 2.5 collective-permute-start.1
  27.1 2.5 fusion.11
  29.7 4.1 %add_convert_fusion.1 = bf16[8192,128]{1,0:T(8,128)(2,1)} fusion(bf16[1,2,32,128,128]{4,3,2,1,0:T(8,128)(2,1)S(1)} %copy-done.3, f32[128]{0:T(128)} %param.18, f32[128]{0:T(128)} %param.17, f32[8192]{0:T(1024)S(1)} %bitcast.118, f32[8192]{0:T(1024)S(1)} %bitcast.113), kind=kLoop, calls=%fused_computation.30 | loop fusion | flops 6291456 | bytes 4260864 | tf_op jit(solution)/shard_map/convert_element_type | solution.py:91
  33.8 5.3 %all-gather.3.cloned.1.call-done = bf16[64,128,128]{2,1,0:T(8,128)(2,1)} async-done(((bf16[16,128,128]{2,1,0:T(8,128)(2,1)}), bf16[64,128,128]{2,1,0:T(8,128)(2,1)}) %all-gather.3.cloned.1.call-update) | async-done | bytes 2097168 | tf_op jit(solution)/shard_map/all_gather | solution.py:80
  39.1 4.5 %copy.68 = bf16[4,16,128,128,1]{2,1,4,3,0:T(8,128)(2,1)} copy(bf16[4,16,128,128,1]{3,2,1,0,4:T(8,128)(2,1)} %bitcast.105) | data formatting | bytes 4194304 | tf_op jit(solution)/shard_map/reshape | solution.py:84
  43.6 4.2 %copy.69 = bf16[64,128,128,1]{1,0,3,2:T(8,128)(2,1)} copy(bf16[64,128,128,1]{2,1,0,3:T(8,128)(2,1)} %bitcast.106) | data formatting | bytes 4194304 | tf_op jit(solution)/shard_map/all_gather | solution.py:80
  47.8 39.8 %all-gather.5.cloned.1.call-done = bf16[64,4,32,128]{3,2,1,0:T(8,128)(2,1)} async-done(((bf16[64,1,32,128]{3,2,1,0:T(8,128)(2,1)}), bf16[64,4,32,128]{3,2,1,0:T(8,128)(2,1)}) %all-gather.5.cloned.1.call-update) | async-done | bytes 2097168 | tf_op jit(solution)/shard_map/all_gather | solution.py:78
  87.6 3.3 gather_fusion
  93.4 7.2 %copy.55 = bf16[4,16,2,32,128]{3,1,2,4,0:T(8,128)(2,1)} copy(bf16[4,16,2,32,128]{4,3,2,1,0:T(8,128)(2,1)} %broadcast_select_fusion.1) | data formatting | bytes 2097152 | tf_op jit(solution)/shard_map/jit(_take)/select_n | solution.py:79
  100.6 5.2 %convert_bitcast_fusion = bf16[4,2,32,128,128]{3,2,1,4,0:T(8,128)(2,1)S(1)} fusion(bf16[4,16,128,128,1]{2,1,4,3,0:T(8,128)(2,1)} %copy.68, bf16[4,16,2,32,128]{3,1,2,4,0:T(8,128)(2,1)} %copy.55), kind=kOutput, calls=%fused_computation.7 | convolution fusion | flops 138412032 | bytes 11534336 | tf_op jit(solution)/shard_map/gksih,gkjh->gsijh/dot_general | solution.py:81
  105.9 5.1 %convert_reduce_fusion = (f32[2,32,128]{2,1,0:T(8,128)S(1)}, f32[2,32,128,128]{2,1,0,3:T(8,128)}) fusion(bf16[4,2,32,128,128]{3,2,1,4,0:T(8,128)(2,1)S(1)} %convert_bitcast_fusion), kind=kLoop, calls=%fused_computation.1 | loop fusion | flops 11526144 | bytes 12615680 | tf_op jit(solution)/shard_map/reduce_sum | solution.py:10
  110.9 5.4 %copy.56 = f32[2,32,128,128]{3,2,1,0:T(8,128)} copy(f32[2,32,128,128]{2,1,0,3:T(8,128)} %get-tuple-element.31) | data formatting | bytes 8388608 | tf_op jit(solution)/shard_map/reduce_sum | solution.py:87
  116.3 2.8 multiply_reduce_fusion.2
  119.8 4.5 %add_convert_fusion = bf16[8192,128]{1,0:T(8,128)(2,1)S(1)} fusion(f32[2,32,128,128]{3,2,1,0:T(8,128)S(1)} %copy-done.2, f32[128]{0:T(128)S(1)} %copy-done.18, f32[128]{0:T(128)S(1)} %copy-done.15, f32[8192]{0:T(1024)S(1)} %bitcast.115, f32[8192]{0:T(1024)S(1)} %bitcast.111), kind=kLoop, calls=%fused_computation.28 | loop fusion | flops 5242880 | bytes 6358016 | tf_op jit(solution)/shard_map/convert_element_type | solution.py:89
  127.3 4.3 %fusion.8 = (bf16[8192,128]{1,0:T(8,128)(2,1)}, bf16[8192,128]{1,0:T(8,128)(2,1)}, bf16[8192,128]{1,0:T(8,128)(2,1)S(1)}) fusion(f32[8192,128]{1,0:T(8,128)S(1)} %fusion.48, bf16[1,2,32,128,128]{4,3,2,1,0:T(8,128)(2,1)S(1)} %copy-done.19, f32[8192]{0:T(1024)S(1)} %bitcast.124, bf16[8192,128]{1,0:T(8,128)(2,1)S(1)} %copy-done.7, ...), kind=kOutput, calls=%fused_computation.14 | convolution fusion | flops 284164096 | bytes 14745600 | tf_op jit(solution)/shard_map/dot_general | solution.py:95
  131.6 6.2 %multiply_reduce_fusion.4 = (f32[8192]{0:T(1024)S(1)}, f32[8192]{0:T(1024)S(1)}, f32[8192,128]{1,0:T(8,128)}) fusion(f32[128]{0:T(128)S(1)} %copy-done.15, f32[8192]{0:T(1024)S(1)} %bitcast.116, f32[8192]{0:T(1024)S(1)} %bitcast.112, f32[2,32,128,128]{3,2,1,0:T(8,128)S(1)} %copy-done.2, bf16[8192,128]{1,0:T(8,128)(2,1)S(1)} %get-tuple-element.43, ...), kind=kOutput, calls=%fused_computation.32 | convolution fusion | flops 274710528 | bytes 10650112 | tf_op jit(solution)/shard_map/dot_general | solution.py:104
  137.8 5.5 %copy.57 = f32[2,32,128,128]{2,1,0,3:T(8,128)} copy(f32[2,32,128,128]{3,2,1,0:T(8,128)} %bitcast.103) | data formatting | bytes 8388608 | tf_op jit(solution)/shard_map/reshape | solution.py:104
  143.3 4.8 %multiply_convert_fusion.1 = bf16[2,32,128,128]{2,1,0,3:T(8,128)(2,1)S(1)} fusion(f32[2,32,128,128]{2,1,0,3:T(8,128)} %copy.57, f32[2,32,128,128]{2,1,0,3:T(8,128)} %get-tuple-element.31, f32[2,32,128]{2,1,0:T(8,128)S(1)} %bitcast.120, f32[2,32,128]{2,1,0:T(8,128)S(1)} %bitcast.121, f32[128]{0:T(128)S(1)} %copy-done.15, f32[2,32,128]{2,1,0:T(8,128)S(1)} %add_rsqrt_fusion, ...), kind=kLoop, calls=%fused_computation.25 | loop fusion | flops 8388608 | bytes 10617344 | tf_op jit(solution)/shard_map/convert_element_type | solution.py:111
  149.5 2.5 convert_bitcast_fusion.3
  152.0 4.7 %copy.59 = bf16[64,2,32,128]{3,1,2,0:T(2,128)(2,1)} copy(bf16[64,2,32,128]{0,2,1,3:T(8,128)(2,1)} %convert_bitcast_fusion.3) | data formatting | bytes 2097152 | tf_op jit(solution)/shard_map/optimization_barrier | solution.py:24
  156.7 2.8 convert_bitcast_fusion.2
  163.6 5.4 %copy.62 = bf16[64,2,32,128]{0,2,3,1:T(8,128)(2,1)} copy(bf16[64,2,32,128]{3,2,0,1:T(8,128)(2,1)} %broadcast_select_fusion) | data formatting | bytes 2097152 | tf_op jit(solution)/shard_map/jit(_take)/select_n | solution.py:79
  169.0 5.5 %convert_bitcast_fusion.1 = bf16[2,64,128,128]{2,1,3,0:T(8,128)(2,1)} fusion(bf16[64,2,32,128]{0,2,3,1:T(8,128)(2,1)} %copy.62, bf16[2,32,128,128]{2,1,0,3:T(8,128)(2,1)} %copy-done.5), kind=kOutput, calls=%fused_computation.24 | convolution fusion | flops 136314880 | bytes 7340032 | tf_op jit(solution)/shard_map/sijh,ksih->skjh/dot_general | solution.py:127
  175.2 7.2 %multiply_reduce_fusion.3 = (f32[8192]{0:T(1024)S(1)}, f32[8192]{0:T(1024)S(1)}, f32[8192,128]{1,0:T(8,128)S(1)}) fusion(f32[128]{0:T(128)S(1)} %copy-done.16, f32[8192]{0:T(1024)S(1)} %bitcast.119, f32[8192]{0:T(1024)S(1)} %bitcast.114, bf16[1,2,32,128,128]{4,3,2,1,0:T(8,128)(2,1)S(1)} %copy-done.3, bf16[8192,128]{1,0:T(8,128)(2,1)} %get-tuple-element.41, ...), kind=kOutput, calls=%fused_computation.31 | convolution fusion | flops 275759104 | bytes 8552960 | tf_op jit(solution)/shard_map/dot_general | solution.py:107
  182.4 5.9 %multiply_convert_fusion = bf16[1,2,32,128,128]{4,3,2,1,0:T(8,128)(2,1)} fusion(f32[1,2,32,128,128]{4,3,2,1,0:T(8,128)S(1)} %bitcast.108, bf16[1,2,32,128,128]{4,3,2,1,0:T(8,128)(2,1)S(1)} %copy-done.3, f32[2,32,128]{2,1,0:T(8,128)S(1)} %bitcast.122, f32[2,32,128]{2,1,0:T(8,128)S(1)} %broadcast_multiply_fusion.5, f32[2,32,128]{2,1,0:T(8,128)S(1)} %bitcast.123, ...), kind=kLoop, calls=%fused_computation.22 | loop fusion | flops 9437184 | bytes 8520192 | tf_op jit(solution)/shard_map/convert_element_type | solution.py:110
  188.3 15.6 %reduce-scatter.3.cloned.1.call-done = bf16[64,1,32,128]{3,2,0,1:T(8,128)(2,1)} async-done(((bf16[64,4,32,128]{3,2,0,1:T(8,128)(2,1)}), bf16[64,1,32,128]{3,2,0,1:T(8,128)(2,1)}) %reduce-scatter.3.cloned.1.call-update) | async-done | bytes 524304 | tf_op jit(solution)/shard_map/reduce_scatter | solution.py:116
  203.9 3.5 all-to-all-start
  207.7 3.8 %fusion.49 = f32[128,128]{1,0:T(8,128)} fusion(bf16[8192,128]{1,0:T(8,128)(2,1)} %copy-done.4, bf16[8192,128]{1,0:T(8,128)(2,1)} %copy-done.9), kind=kOutput, calls=%fused_computation.112 | convolution fusion | flops 268435456 | bytes 4259840 | tf_op jit(solution)/shard_map/dot_general | solution.py:101
  212.9 3.3 all-to-all-done
  216.4 33.9 %reduce-scatter.5.cloned.1.call-done = bf16[2,16,128,128]{2,1,3,0:T(8,128)(2,1)} async-done(((bf16[2,64,128,128]{2,1,3,0:T(8,128)(2,1)}), bf16[2,16,128,128]{2,1,3,0:T(8,128)(2,1)}) %reduce-scatter.5.cloned.1.call-update) | async-done | bytes 1048592 | tf_op jit(solution)/shard_map/reduce_scatter | solution.py:131
  253.2 3.6 multiply_convert_fusion.6
  262.3 89.8 %all-reduce.3.cloned.1.call-done = (f32[128,512]{1,0:T(8,128)}, f32[128,128]{1,0:T(8,128)}, f32[128,128]{1,0:T(8,128)}) async-done(((f32[128,512]{1,0:T(8,128)}, f32[128,128]{1,0:T(8,128)}, f32[128,128]{1,0:T(8,128)}), (f32[128,512]{1,0:T(8,128)}, f32[128,128]{1,0:T(8,128)}, f32[128,128]{1,0:T(8,128)})) %all-reduce.3.cloned.1.call-update) | async-done | bytes 393232 | tf_op jit(solution)/shard_map/psum | solution.py:151
  (103 shorter events, 43.6 us)
Async XLA Ops:
  7.2 1.7 copy-start
  7.2 31.9 %all-gather.3.cloned.1.call-start = ((), (), s32[]{:S(2)}) async-start(), calls=%async_computation.3 | async-start | bytes 2621440 | tf_op jit(solution)/shard_map/all_gather | solution.py:80
  10.4 1.9 copy-start.1
  12.3 13.5 %copy-start.3 = (bf16[1,2,32,128,128]{4,3,2,1,0:T(8,128)(2,1)S(1)}, bf16[1,2,32,128,128]{4,3,2,1,0:T(8,128)(2,1)}, u32[]{:S(2)}) copy-start(bf16[1,2,32,128,128]{4,3,2,1,0:T(8,128)(2,1)} %param.13) | copy-start | bytes 6291460
  13.7 73.9 %all-gather.5.cloned.1.call-start = ((), (), s32[]{:S(2)}) async-start(), calls=%async_computation.4 | async-start | bytes 2621440 | tf_op jit(solution)/shard_map/all_gather | solution.py:78
  14.5 0.8 copy-start.11
  15.3 4.5 %collective-permute-start = (bf16[16,1,32,128]{3,2,1,0:T(8,128)(2,1)}, bf16[16,1,32,128]{3,2,1,0:T(8,128)(2,1)S(1)}, u32[]{:S(2)}, u32[]{:S(2)}) collective-permute-start(bf16[16,1,32,128]{3,2,1,0:T(8,128)(2,1)} %get-tuple-element.54), channel_id=1, source_target_pairs={{0,1},{1,0},{2,3},{3,2},{4,5},{5,4},{6,7},{7,6},{8,9},{9,8},{10,11... | collective-permute-start | bytes 393224 | tf_op jit(solution)/shard_map/ppermute | solution.py:75
  15.8 6.8 %collective-permute-start.1 = (bf16[16,1,32,128]{3,2,1,0:T(8,128)(2,1)S(1)}, bf16[16,1,32,128]{3,2,1,0:T(8,128)(2,1)S(1)}, u32[]{:S(2)}, u32[]{:S(2)}) collective-permute-start(bf16[16,1,32,128]{3,2,1,0:T(8,128)(2,1)S(1)} %get-tuple-element.53), channel_id=1, source_target_pairs={{0,2},{1,3},{2,0},{3,1},{4,6},{5,7},{6,4},{7,5},{8,10},{9,11},{10,... | collective-permute-start | bytes 393224 | tf_op jit(solution)/shard_map/ppermute | solution.py:75
  18.3 6.8 %collective-permute-start.2 = (bf16[16,1,32,128]{3,2,1,0:T(8,128)(2,1)S(1)}, bf16[16,1,32,128]{3,2,1,0:T(8,128)(2,1)S(1)}, u32[]{:S(2)}, u32[]{:S(2)}) collective-permute-start(bf16[16,1,32,128]{3,2,1,0:T(8,128)(2,1)S(1)} %get-tuple-element.52), channel_id=1, source_target_pairs={{0,3},{1,2},{2,1},{3,0},{4,7},{5,6},{6,5},{7,4},{8,11},{9,10},{10,... | collective-permute-start | bytes 393224 | tf_op jit(solution)/shard_map/ppermute | solution.py:75
  25.8 178.2 %reduce-scatter.3.cloned.1.call-start = ((), (), s32[]{:S(2)}) async-start(), calls=%async_computation.5 | async-start | bytes 2621440 | tf_op jit(solution)/shard_map/reduce_scatter | solution.py:116
  116.3 3.4 copy-start.2
  116.3 3.4 copy-start.15
  116.3 3.5 copy-start.18
  119.1 5.2 %copy-start.14 = (bf16[128,128]{1,0:T(8,128)(2,1)S(1)}, bf16[128,128]{1,0:T(8,128)(2,1)}, u32[]{:S(2)}) copy-start(bf16[128,128]{1,0:T(8,128)(2,1)} %param.22) | copy-start | bytes 98308
  124.3 1.3 copy-start.4
  124.3 2.3 copy-start.7
  124.3 3.0 copy-start.19
  124.3 3.0 copy-start.20
  131.6 6.2 %copy-start.9 = (bf16[8192,128]{1,0:T(8,128)(2,1)}, bf16[8192,128]{1,0:T(8,128)(2,1)S(1)}, u32[]{:S(2)}) copy-start(bf16[8192,128]{1,0:T(8,128)(2,1)S(1)} %get-tuple-element.43) | copy-start | bytes 6291460
  143.3 6.1 %copy-start.6 = (bf16[64,128,128,1]{1,0,3,2:T(8,128)(2,1)S(1)}, bf16[64,128,128,1]{1,0,3,2:T(8,128)(2,1)}, u32[]{:S(2)}) copy-start(bf16[64,128,128,1]{1,0,3,2:T(8,128)(2,1)} %copy.69) | copy-start | bytes 6291460
  148.1 1.4 copy-start.5
  149.4 7.2 %copy-start.21 = (s32[1,2]{1,0:T(1,128)S(1)}, s32[1,2]{1,0:T(1,128)}, u32[]{:S(2)}) copy-start(s32[1,2]{1,0:T(1,128)} %param.15) | copy-start | bytes 28
  161.2 89.1 %reduce-scatter.5.cloned.1.call-start = ((), (), s32[]{:S(2)}) async-start(), calls=%async_computation.6 | async-start | bytes 5242880 | tf_op jit(solution)/shard_map/reduce_scatter | solution.py:131
  174.5 0.7 copy-start.16
  188.3 23.2 %copy-start.8 = (bf16[8192,128]{1,0:T(8,128)(2,1)S(1)}, bf16[8192,128]{1,0:T(8,128)(2,1)}, u32[]{:S(2)}) copy-start(bf16[8192,128]{1,0:T(8,128)(2,1)} %add_convert_fusion.1) | copy-start | bytes 6291460
  203.9 12.3 %all-to-all-start = ((bf16[4,16,32,128]{3,2,1,0:T(8,128)(2,1)}), bf16[4,16,32,128]{3,2,1,0:T(8,128)(2,1)S(1)}, u32[]{:S(2)}, u32[]{:S(2)}) async-start(bf16[4,16,32,128]{3,2,1,0:T(8,128)(2,1)} %bitcast.117), calls=%async_computation.1 | async-start | bytes 1048576 | tf_op jit(solution)/shard_map/all_to_all | solution.py:119
  207.4 144.7 %all-reduce.3.cloned.1.call-start = ((), (), s32[]{:S(2)}) async-start(), calls=%async_computation.7 | async-start | bytes 786432 | tf_op jit(solution)/shard_map/psum | solution.py:151
  207.7 3.8 %copy-start.10 = (bf16[8192,128]{1,0:T(8,128)(2,1)S(1)}, bf16[8192,128]{1,0:T(8,128)(2,1)}, u32[]{:S(2)}) copy-start(bf16[8192,128]{1,0:T(8,128)(2,1)} %get-tuple-element.41) | copy-start | bytes 6291460
  253.2 4.4 %copy-start.17 = (f32[128]{0:T(128)S(1)}, f32[128]{0:T(128)}, u32[]{:S(2)}) copy-start(f32[128]{0:T(128)} %param.18) | copy-start | bytes 1540
  256.9 0.8 copy-start.13
  256.9 2.0 copy-start.12
Sparse Core Ops, SparseCore 0:
  13.8 25.2 all-gather.2
  41.3 46.3 all-gather.4
  161.3 42.5 reduce-scatter.2
  206.5 43.8 reduce-scatter.4
  261.1 90.9 all-reduce.2
